TPU v7x, 32 devices: a whole 2x2x4 slice. The times are simulated.
32 devices in a mesh: dp: 4 (over y, x), expert: 8 (over z, core).
Axes of the slice: x: 2, y: 2, z: 4, core: 2. Of those that a mesh axis runs over, the one named last changes fastest.
Arguments:
- tokens: bfloat16 [4096, 2048], P(('dp', 'expert')), may hold values from -6 to 6
- expert_ids: int32 [4096, 2], P(('dp', 'expert')), may hold values from 0 to 7, all different within a row; in each aligned block of 128 rows (0 to 127, 128 to 255, ...) at most 48 rows name the same one
- gates: bfloat16 [4096, 2], P(('dp', 'expert')), may hold values from 0.049804688 to 1
- cotangent: bfloat16 [4096, 2048], P(('dp', 'expert')), may hold values from -6 to 6
- w_gate: bfloat16 [8, 2048, 768], P('expert'), may hold values from -0.125 to 0.125
- w_up: bfloat16 [8, 2048, 768], P('expert'), may hold values from -0.125 to 0.125
- w_down: bfloat16 [8, 768, 2048], P('expert'), may hold values from -0.21875 to 0.21875
Outputs:
- grad_tokens: bfloat16 [4096, 2048], P(('dp', 'expert'))
- grad_gates: bfloat16 [4096, 2], P(('dp', 'expert'))
- grad_w_gate: bfloat16 [8, 2048, 768], P('expert', 'dp')
- grad_w_up: bfloat16 [8, 2048, 768], P('expert', 'dp')
- grad_w_down: bfloat16 [8, 768, 2048], P('expert', None, 'dp')
Inputs may be any that keep to these rules, and one draw needn't show every extreme that they name: `expert_ids`: within the 128 rows of one device no expert is named by more than 48 rows, and in some of these aligned blocks an expert is named by exactly 48 rows.
All inputs are finite; a program needn't handle non-finite values.
Results may differ from a plain program's by a relative error of at most 0.013.
Values may be sent and summed in bfloat16 or wider, within the bound.
A program may use at most 128 MiB of HBM per device.

v0:
```python
import jax
import jax.numpy as jnp
from jax import lax
from jax.sharding import PartitionSpec as P


def contract_rows(left, right):
    return lax.dot_general(
        left, right, (((0,), (0,)), ((), ())), preferred_element_type=jnp.float32
    )


def expert_pass(rows, cot_rows, gate_column, gate_mat, up_mat, down_mat):
    pre_gate = jnp.dot(rows, gate_mat, preferred_element_type=jnp.float32)
    pre_up = jnp.dot(rows, up_mat, preferred_element_type=jnp.float32)
    sigmoid_gate = jax.nn.sigmoid(pre_gate)
    activated = pre_gate * sigmoid_gate
    hidden = (activated * pre_up).astype(jnp.bfloat16)
    expert_out = jnp.dot(hidden, down_mat, preferred_element_type=jnp.float32)
    cot_float = cot_rows.astype(jnp.float32)
    score_grad = jnp.sum(expert_out * cot_float, axis=1)
    scaled = (gate_column.astype(jnp.float32)[:, None] * cot_float).astype(jnp.bfloat16)
    grad_hidden = jnp.dot(scaled, down_mat.T, preferred_element_type=jnp.float32)
    grad_pre_gate = (
        grad_hidden * pre_up * sigmoid_gate * (1.0 + pre_gate * (1.0 - sigmoid_gate))
    ).astype(jnp.bfloat16)
    grad_pre_up = (grad_hidden * activated).astype(jnp.bfloat16)
    row_grad = (
        jnp.dot(grad_pre_gate, gate_mat.T, preferred_element_type=jnp.float32)
        + jnp.dot(grad_pre_up, up_mat.T, preferred_element_type=jnp.float32)
    ).astype(jnp.bfloat16)
    return (hidden, scaled, grad_pre_gate, grad_pre_up, row_grad, score_grad)


def by_owner(values, owners, capacity):
    return values.reshape((owners, capacity) + values.shape[1:])


def sum_weights(part_gate, part_up, part_down):
    return (
        lax.psum_scatter(
            part_gate.astype(jnp.bfloat16), "dp", scatter_dimension=0, tiled=True
        ).astype(jnp.float32),
        lax.psum_scatter(
            part_up.astype(jnp.bfloat16), "dp", scatter_dimension=0, tiled=True
        ).astype(jnp.float32),
        lax.psum_scatter(
            part_down.astype(jnp.bfloat16), "dp", scatter_dimension=1, tiled=True
        ).astype(jnp.float32),
    )


def send_back(row_grad, score_grad, owners, capacity):
    score_half = score_grad.astype(jnp.bfloat16)
    back_rows = lax.all_to_all(
        by_owner(row_grad, owners, capacity), "expert", split_axis=0, concat_axis=0, tiled=True
    )
    back_scores = lax.all_to_all(
        by_owner(score_half, owners, capacity), "expert", split_axis=0, concat_axis=0, tiled=True
    )
    return (back_rows, back_scores)


def body(tokens, expert_ids, gates, cotangent, w_gate, w_up, w_down):
    tok_rows, model_width = tokens.shape
    top_count = expert_ids.shape[1]
    owners = lax.axis_size("expert")
    capacity = min(tok_rows, 3 * tok_rows * top_count // (2 * owners))
    slot_count = owners * capacity
    flat_ids = expert_ids.reshape(-1)
    pair_count = flat_ids.shape[0]
    picked = (flat_ids[:, None] == jnp.arange(owners, dtype=jnp.int32)[None, :]).astype(jnp.int32)
    before = jnp.cumsum(picked, axis=0) - picked
    position = jnp.sum(before * picked, axis=1)
    target = flat_ids * capacity + position
    source_row = jnp.arange(pair_count, dtype=jnp.int32) // top_count
    send_rows = (
        jnp.zeros((slot_count, model_width), jnp.bfloat16).at[target].set(tokens[source_row])
    )
    send_cot = (
        jnp.zeros((slot_count, model_width), jnp.bfloat16).at[target].set(cotangent[source_row])
    )
    send_gate = jnp.zeros((slot_count,), jnp.bfloat16).at[target].set(gates.reshape(-1))
    recv_gate = lax.all_to_all(
        by_owner(send_gate, owners, capacity), "expert", split_axis=0, concat_axis=0, tiled=True
    )
    recv_rows = lax.all_to_all(
        by_owner(send_rows, owners, capacity), "expert", split_axis=0, concat_axis=0, tiled=True
    )
    recv_cot = lax.all_to_all(
        by_owner(send_cot, owners, capacity), "expert", split_axis=0, concat_axis=0, tiled=True
    )
    rows = recv_rows.reshape(slot_count, model_width)
    cot_rows = recv_cot.reshape(slot_count, model_width)
    gate_column = recv_gate.reshape(slot_count)
    hidden, scaled, grad_pre_gate, grad_pre_up, row_grad, score_grad = expert_pass(
        rows, cot_rows, gate_column, w_gate[0], w_up[0], w_down[0]
    )
    part_gate = contract_rows(rows, grad_pre_gate)
    part_up = contract_rows(rows, grad_pre_up)
    part_down = contract_rows(hidden, scaled)
    back_rows, back_scores = send_back(row_grad, score_grad, owners, capacity)
    summed = sum_weights(part_gate, part_up, part_down)
    pair_rows = back_rows.reshape(slot_count, model_width)[target].reshape(
        tok_rows, top_count, model_width
    )
    grad_tokens = jnp.sum(pair_rows.astype(jnp.float32), axis=1).astype(jnp.bfloat16)
    grad_gates = back_scores.reshape(slot_count)[target].reshape(tok_rows, top_count)
    grad_w_gate = summed[0].astype(jnp.bfloat16)[None]
    grad_w_up = summed[1].astype(jnp.bfloat16)[None]
    grad_w_down = summed[2].astype(jnp.bfloat16)[None]
    return (grad_tokens, grad_gates, grad_w_gate, grad_w_up, grad_w_down)


def solution(mesh):
    placed = (
        P(("dp", "expert"), None),
        P(("dp", "expert"), None),
        P(("dp", "expert"), None),
        P(("dp", "expert"), None),
        P("expert", None, None),
        P("expert", None, None),
        P("expert", None, None),
    )
    return jax.shard_map(
        body,
        mesh=mesh,
        in_specs=placed,
        out_specs=(
            P(("dp", "expert"), None),
            P(("dp", "expert"), None),
            P("expert", "dp", None),
            P("expert", "dp", None),
            P("expert", None, "dp"),
        ),
        check_vma=False,
    )
```

profile of v0, /device:TPU:0, one launch (start us, length us, event | category | flops | bytes accessed | tf_op | source)
XLA Modules:
  0.0 270.8 jit_solution(3574319315359718348)
XLA Ops:
  7.2 0.0 copy-start
  7.2 0.8 broadcast_multiply_fusion
  8.0 0.9 copy.24
  8.9 0.1 eq.29
  9.1 0.1 eq.25
  9.2 0.8 copy.26
  10.0 0.1 reshape.216
  10.1 0.1 copy.23
  10.2 0.1 mul.58
  10.4 0.6 reduce-window.6
  11.0 0.2 slice_reduce_fusion
  11.2 0.1 fusion.27
  11.4 2.2 scatter_custom_fusion
  13.5 0.7 all_to_all.25
  14.2 6.3 %all-to-all-start = ((bf16[8,1,48]{2,1,0:T(2,128)(2,1)}), bf16[8,1,48]{2,1,0:T(2,128)(2,1)S(1)}, u32[]{:S(2)}, u32[]{:S(2)}) async-start(bf16[8,1,48]{2,1,0:T(2,128)(2,1)} %all_to_all.25), calls=%async_computation | async-start | bytes 8192 | tf_op jit(solution)/shard_map/all_to_all | solution.py:84
  20.6 6.8 %scatter_custom_fusion.2 = bf16[384,2048]{1,0:T(8,128)(2,1)} fusion(s32[256]{0:T(256)S(1)} %bitcast.70, bf16[128,2048]{1,0:T(8,128)(2,1)} %param.7, s32[1024]{0:T(1024)S(1)} %pad_clamp_fusion.1, bf16[]{:T(256)} %constant.27.clone.1), kind=kCustom, calls=%fused_computation.34 | custom fusion | bytes 1573376 | tf_op jit(solution)/shard_map/scatter | solution.py:78
  27.4 0.0 all-to-all-done
  27.4 5.1 %all-to-all-start.2 = ((bf16[8,48,2048]{2,1,0:T(8,128)(2,1)}), bf16[8,48,2048]{2,1,0:T(8,128)(2,1)}, u32[]{:S(2)}, u32[]{:S(2)}) async-start(bf16[8,48,2048]{2,1,0:T(8,128)(2,1)} %bitcast.65), calls=%async_computation.2 | async-start | bytes 3145728 | tf_op jit(solution)/shard_map/all_to_all | solution.py:87
  32.5 6.9 %scatter_custom_fusion.1 = bf16[384,2048]{1,0:T(8,128)(2,1)} fusion(s32[256]{0:T(256)S(1)} %bitcast.71, bf16[128,2048]{1,0:T(8,128)(2,1)} %param.10, s32[1024]{0:T(1024)S(1)} %pad_clamp_fusion.1, bf16[]{:T(256)} %constant.27.clone.1), kind=kCustom, calls=%fused_computation.36 | custom fusion | bytes 1573376 | tf_op jit(solution)/shard_map/scatter | solution.py:81
  39.4 31.1 %all-to-all-done.2 = bf16[8,48,2048]{2,1,0:T(8,128)(2,1)} async-done(((bf16[8,48,2048]{2,1,0:T(8,128)(2,1)}), bf16[8,48,2048]{2,1,0:T(8,128)(2,1)}, u32[]{:S(2)}, u32[]{:S(2)}) %all-to-all-start.2) | async-done | bytes 1572896 | tf_op jit(solution)/shard_map/all_to_all | solution.py:87
  70.4 4.3 %all-to-all-start.1 = ((bf16[8,48,2048]{2,1,0:T(8,128)(2,1)}), bf16[8,48,2048]{2,1,0:T(8,128)(2,1)}, u32[]{:S(2)}, u32[]{:S(2)}) async-start(bf16[8,48,2048]{2,1,0:T(8,128)(2,1)} %bitcast.64), calls=%async_computation.1 | async-start | bytes 3145728 | tf_op jit(solution)/shard_map/all_to_all | solution.py:90
  74.7 0.0 reduce-scatter.8.cloned.1.call-start
  74.8 0.1 reshape.179
  74.9 4.8 %fusion.5 = f32[384,768]{1,0:T(8,128)} fusion(bf16[384,2048]{1,0:T(8,128)(2,1)} %bitcast.10, bf16[1,2048,768]{2,1,0:T(8,128)(2,1)} %param.11), kind=kOutput, calls=%fused_computation.18 | convolution fusion | flops 1207959552 | bytes 5898240 | tf_op jit(solution)/shard_map/dot_general | solution.py:14
  79.7 32.9 %all-to-all-done.1 = bf16[8,48,2048]{2,1,0:T(8,128)(2,1)} async-done(((bf16[8,48,2048]{2,1,0:T(8,128)(2,1)}), bf16[8,48,2048]{2,1,0:T(8,128)(2,1)}, u32[]{:S(2)}, u32[]{:S(2)}) %all-to-all-start.1) | async-done | bytes 1572896 | tf_op jit(solution)/shard_map/all_to_all | solution.py:90
  112.6 0.0 copy-start.1
  112.6 1.9 fusion
  114.4 0.5 copy-done.1
  114.9 0.0 copy-start.4
  114.9 1.4 fusion.13
  116.4 0.0 copy-done
  116.4 0.0 copy-done.4
  116.4 4.2 %multiply_convert_fusion = (bf16[384,768]{1,0:T(8,128)(2,1)S(1)}, bf16[384,768]{1,0:T(8,128)(2,1)}, bf16[384,768]{1,0:T(8,128)(2,1)}) fusion(f32[384,768]{1,0:T(8,128)S(1)} %copy-done.4, f32[384,768]{1,0:T(8,128)S(1)} %fusion.13, bf16[384,2048]{1,0:T(8,128)(2,1)} %bitcast.10, bf16[1,2048,768]{2,1,0:T(8,128)(2,1)S(1)} %copy-done), kind=kOutput, calls=%fused_computation.29 | convolution fusion | flops 1212383232 | bytes 8847360 | tf_op jit(solution)/shard_map/dot_general | solution.py:15
  120.6 0.0 copy-start.3
  120.6 1.9 fusion.2
  122.6 0.0 copy-done.3
  122.6 3.5 %convolution_convert_fusion = bf16[768,2048]{1,0:T(8,128)(2,1)} fusion(bf16[384,768]{1,0:T(8,128)(2,1)S(1)} %get-tuple-element.20, bf16[384,2048]{1,0:T(8,128)(2,1)S(1)} %fusion.2), kind=kOutput, calls=%fused_computation.7 | convolution fusion | flops 1209532416 | bytes 5308416 | tf_op jit(solution)/shard_map/dot_general | solution.py:8
  126.1 0.0 reduce-scatter.8.cloned.1.call-update
  126.1 0.3 reduce-scatter.4.cloned.1.call-start
  126.4 5.0 %convolution_convert_fusion.2 = bf16[2048,768]{1,0:T(8,128)(2,1)} fusion(bf16[384,2048]{1,0:T(8,128)(2,1)} %bitcast.10, bf16[384,768]{1,0:T(8,128)(2,1)} %get-tuple-element.21), kind=kOutput, calls=%fused_computation.9 | convolution fusion | flops 1209532416 | bytes 5308416 | tf_op jit(solution)/shard_map/dot_general | solution.py:8
  131.4 0.0 reduce-scatter.4.cloned.1.call-update
  131.5 0.0 reduce-scatter.6.cloned.1.call-start
  131.5 5.1 %convolution_convert_fusion.1 = bf16[2048,768]{1,0:T(8,128)(2,1)} fusion(bf16[384,2048]{1,0:T(8,128)(2,1)} %bitcast.10, bf16[384,768]{1,0:T(8,128)(2,1)} %get-tuple-element.22), kind=kOutput, calls=%fused_computation.8 | convolution fusion | flops 1209532416 | bytes 5308416 | tf_op jit(solution)/shard_map/dot_general | solution.py:8
  136.7 0.0 reduce-scatter.6.cloned.1.call-update
  136.7 4.2 %fusion.1 = bf16[384]{0:T(512)(128)(2,1)S(1)} fusion(bf16[8,48,2048]{2,1,0:T(8,128)(2,1)} %all-to-all-done.1, bf16[384,768]{1,0:T(8,128)(2,1)} %copy-done.3, bf16[1,768,2048]{2,1,0:T(8,128)(2,1)} %param.13), kind=kOutput, calls=%fused_computation.14 | convolution fusion | flops 1210318464 | bytes 5309184 | tf_op jit(solution)/shard_map/dot_general | solution.py:19
  140.9 0.7 convert_element_type.107
  141.6 3.3 %all-to-all-start.4 = ((bf16[8,1,48]{2,1,0:T(2,128)(2,1)}), bf16[8,1,48]{2,1,0:T(2,128)(2,1)S(1)}, u32[]{:S(2)}, u32[]{:S(2)}) async-start(bf16[8,1,48]{2,1,0:T(2,128)(2,1)} %convert_element_type.107), calls=%async_computation.4 | async-start | bytes 8192 | tf_op jit(solution)/shard_map/all_to_all | solution.py:58
  144.9 0.0 copy-start.2
  144.9 3.6 %fusion.3 = f32[384,2048]{1,0:T(8,128)S(1)} fusion(bf16[384,768]{1,0:T(8,128)(2,1)} %get-tuple-element.21, bf16[1,2048,768]{2,1,0:T(8,128)(2,1)} %param.11), kind=kOutput, calls=%fused_computation.16 | convolution fusion | flops 1207959552 | bytes 6881280 | tf_op jit(solution)/shard_map/dot_general | solution.py:29
  148.5 0.0 copy-done.2
  148.5 2.6 add_convert_fusion
  151.1 0.0 all-to-all-done.4
  151.1 5.0 %all-to-all-start.3 = ((bf16[8,48,2048]{2,1,0:T(8,128)(2,1)}), bf16[8,48,2048]{2,1,0:T(8,128)(2,1)}, u32[]{:S(2)}, u32[]{:S(2)}) async-start(bf16[8,48,2048]{2,1,0:T(8,128)(2,1)} %bitcast.66), calls=%async_computation.3 | async-start | bytes 3145728 | tf_op jit(solution)/shard_map/all_to_all | solution.py:55
  156.1 0.1 reshape.175
  156.2 1.9 gather_fusion.1
  158.1 0.2 reshape.176
  158.3 0.6 copy.29
  158.9 35.1 %all-to-all-done.3 = bf16[8,48,2048]{2,1,0:T(8,128)(2,1)} async-done(((bf16[8,48,2048]{2,1,0:T(8,128)(2,1)}), bf16[8,48,2048]{2,1,0:T(8,128)(2,1)}, u32[]{:S(2)}, u32[]{:S(2)}) %all-to-all-start.3) | async-done | bytes 1572896 | tf_op jit(solution)/shard_map/all_to_all | solution.py:55
  194.0 4.9 %gather_fusion = bf16[256,2048]{1,0:T(8,128)(2,1)} fusion(bf16[384,2048]{1,0:T(8,128)(2,1)} %bitcast.14, s32[1024]{0:T(1024)S(1)} %pad_clamp_fusion), kind=kCustom, calls=%fused_computation.2 | custom fusion | bytes 2098176 | tf_op jit(solution)/shard_map/gather | solution.py:104
  198.9 2.5 reshape.174
  201.5 4.6 %reduce_sum.34 = bf16[128,2048]{1,0:T(8,128)(2,1)} reduce(bf16[128,2,2048]{2,1,0:T(2,128)(2,1)} %reshape.174, bf16[]{:T(256)} %constant.27.clone.1), dimensions={1}, to_apply=%region_6.7 | reduce | flops 262144 | bytes 1572866 | tf_op jit(solution)/shard_map/reduce_sum | solution.py:107
  206.1 0.0 reduce-scatter.8.cloned.1.call-done
  206.1 10.6 %reduce-scatter.4.cloned.1.call-done = bf16[512,768]{1,0:T(8,128)(2,1)} async-done(((bf16[2048,768]{1,0:T(8,128)(2,1)}), bf16[512,768]{1,0:T(8,128)(2,1)}) %reduce-scatter.4.cloned.1.call-update) | async-done | bytes 786448 | tf_op jit(solution)/shard_map/reduce_scatter | solution.py:41
  216.7 47.5 %reduce-scatter.6.cloned.1.call-done = bf16[512,768]{1,0:T(8,128)(2,1)} async-done(((bf16[2048,768]{1,0:T(8,128)(2,1)}), bf16[512,768]{1,0:T(8,128)(2,1)}) %reduce-scatter.6.cloned.1.call-update) | async-done | bytes 786448 | tf_op jit(solution)/shard_map/reduce_scatter | solution.py:44
  (10 shorter events, 0.1 us)
Async XLA Ops:
  7.2 109.2 %copy-start = (bf16[1,2048,768]{2,1,0:T(8,128)(2,1)S(1)}, bf16[1,2048,768]{2,1,0:T(8,128)(2,1)}, u32[]{:S(2)}) copy-start(bf16[1,2048,768]{2,1,0:T(8,128)(2,1)} %param.12) | copy-start | bytes 9437188
  14.2 13.2 %all-to-all-start = ((bf16[8,1,48]{2,1,0:T(2,128)(2,1)}), bf16[8,1,48]{2,1,0:T(2,128)(2,1)S(1)}, u32[]{:S(2)}, u32[]{:S(2)}) async-start(bf16[8,1,48]{2,1,0:T(2,128)(2,1)} %all_to_all.25), calls=%async_computation | async-start | bytes 8192 | tf_op jit(solution)/shard_map/all_to_all | solution.py:84
  27.4 43.0 %all-to-all-start.2 = ((bf16[8,48,2048]{2,1,0:T(8,128)(2,1)}), bf16[8,48,2048]{2,1,0:T(8,128)(2,1)}, u32[]{:S(2)}, u32[]{:S(2)}) async-start(bf16[8,48,2048]{2,1,0:T(8,128)(2,1)} %bitcast.65), calls=%async_computation.2 | async-start | bytes 3145728 | tf_op jit(solution)/shard_map/all_to_all | solution.py:87
  70.4 42.2 %all-to-all-start.1 = ((bf16[8,48,2048]{2,1,0:T(8,128)(2,1)}), bf16[8,48,2048]{2,1,0:T(8,128)(2,1)}, u32[]{:S(2)}, u32[]{:S(2)}) async-start(bf16[8,48,2048]{2,1,0:T(8,128)(2,1)} %bitcast.64), calls=%async_computation.1 | async-start | bytes 3145728 | tf_op jit(solution)/shard_map/all_to_all | solution.py:90
  74.7 131.3 %reduce-scatter.8.cloned.1.call-start = ((), (), s32[]{:S(2)}) async-start(), calls=%async_computation.10 | async-start | bytes 3932160 | tf_op jit(solution)/shard_map/reduce_scatter | solution.py:47
  112.6 2.4 copy-start.1
  114.9 1.5 copy-start.4
  120.6 1.9 copy-start.3
  126.1 90.6 %reduce-scatter.4.cloned.1.call-start = ((), (), s32[]{:S(2)}) async-start(), calls=%async_computation.8 | async-start | bytes 3932160 | tf_op jit(solution)/shard_map/reduce_scatter | solution.py:41
  131.5 132.8 %reduce-scatter.6.cloned.1.call-start = ((), (), s32[]{:S(2)}) async-start(), calls=%async_computation.9 | async-start | bytes 3932160 | tf_op jit(solution)/shard_map/reduce_scatter | solution.py:44
  141.6 9.5 %all-to-all-start.4 = ((bf16[8,1,48]{2,1,0:T(2,128)(2,1)}), bf16[8,1,48]{2,1,0:T(2,128)(2,1)S(1)}, u32[]{:S(2)}, u32[]{:S(2)}) async-start(bf16[8,1,48]{2,1,0:T(2,128)(2,1)} %convert_element_type.107), calls=%async_computation.4 | async-start | bytes 8192 | tf_op jit(solution)/shard_map/all_to_all | solution.py:58
  144.9 3.6 %copy-start.2 = (bf16[384,768]{1,0:T(8,128)(2,1)S(1)}, bf16[384,768]{1,0:T(8,128)(2,1)}, u32[]{:S(2)}) copy-start(bf16[384,768]{1,0:T(8,128)(2,1)} %get-tuple-element.22) | copy-start | bytes 1769476
  151.1 42.9 %all-to-all-start.3 = ((bf16[8,48,2048]{2,1,0:T(8,128)(2,1)}), bf16[8,48,2048]{2,1,0:T(8,128)(2,1)}, u32[]{:S(2)}, u32[]{:S(2)}) async-start(bf16[8,48,2048]{2,1,0:T(8,128)(2,1)} %bitcast.66), calls=%async_computation.3 | async-start | bytes 3145728 | tf_op jit(solution)/shard_map/all_to_all | solution.py:55
Sparse Core Ops, SparseCore 0:
  126.3 42.8 reduce-scatter.7
  172.7 43.9 reduce-scatter.3
  220.3 43.9 reduce-scatter.5
where the time goes:
time: 272 us; the launch traced here: 271 us
  waiting for transfers between devices  157 us (58%)
  matrix products  34.5 us (13%)
  local copies, waits for them, and re-layouts  30.7 us (11%)
  starting transfers between devices  24.4 us (9%)
  between operations  13.9 us (5%)
  other arithmetic  10 us (4%)
    reduce_scatter x1, waiting for transfers between devices, sum_weights(): lax.psum_scatter(part_up.astype(jnp.bfloat16), 'dp', scatter_dimension=0,...  47.5 us
    all_to_all x1, waiting for transfers between devices, send_back(): lax.all_to_all(by_owner(row_grad, owners, capacity), 'expert', split_axis...  35.1 us
    all_to_all x1, waiting for transfers between devices, body(): lax.all_to_all(by_owner(send_cot, owners, capacity), 'expert', split_axis...  32.9 us
    all_to_all x1, waiting for transfers between devices, body(): lax.all_to_all(by_owner(send_rows, owners, capacity), 'expert', split_axi...  31.1 us
    dot_general x3, matrix products, contract_rows(): lax.dot_general(left, right, (((0,), (0,)), ((), ())), preferred_element_...  13.7 us
    scatter x2, local copies, waits for them, and re-layouts, body(): jnp.zeros((slot_count, model_width), jnp.bfloat16).at[target]  13.7 us
    reduce_scatter x1, waiting for transfers between devices, sum_weights(): lax.psum_scatter(part_gate.astype(jnp.bfloat16), 'dp', scatter_dimension=...  10.6 us
    all_to_all x1, starting transfers between devices, body(): lax.all_to_all(by_owner(send_gate, owners, capacity), 'expert', split_axi...  6.33 us
  transfers between devices with their start and end apart: 8, of which 5 were waited for; matrix products, arithmetic and copies ran while one was open for 20% of the time, Pallas kernels for 0%

commit v1 on v0

--- a/solution.py
+++ b/solution.py
@@ -1,7 +1,367 @@
+import functools
+
 import jax
 import jax.numpy as jnp
 from jax import lax
+from jax.experimental import pallas as pl
+from jax.experimental.pallas import tpu as pltpu
 from jax.sharding import PartitionSpec as P
+
+MESH = pl.DeviceIdType.MESH
+F32 = jnp.float32
+BF16 = jnp.bfloat16
+
+
+def tile_of(size, most):
+    step = min(size, most)
+    while size % step:
+        step -= 128
+    return step
+
+
+def dot_nt(left, right):
+    return lax.dot_general(left, right, (((1,), (1,)), ((), ())), preferred_element_type=F32)
+
+
+def dot_tn(left, right):
+    return lax.dot_general(left, right, (((0,), (0,)), ((), ())), preferred_element_type=F32)
+
+
+def layer_kernel(
+    owners, groups, capacity,
+    ids_ref, gates_ref, tok_ref, cot_ref, wg_hbm, wu_hbm, wd_hbm,
+    gtok_ref, ggate_ref, gwg_ref, gwu_ref, gwd_ref,
+    wg, wu, wd, w_sem,
+    pick, gate_col, send_tok, send_cot, rows, scaled, pre_gate, pre_up, score,
+    x_rows, x_scaled, x_hid, x_gg, x_gu, own_sem,
+    back_send, back_recv, score_send, score_recv, acc_gate, acc_up,
+    tok_s, tok_r, cot_s, cot_r, back_s, back_r, sc_s, sc_r,
+    fr_s, fr_r, fc_s, fc_r, h_s, h_r, gg_s, gg_r, gu_s, gu_r,
+):
+    me = lax.axis_index("expert")
+    grp = lax.axis_index("dp")
+    tok_count, width = tok_ref.shape
+    slots = owners * capacity
+    hid_width = wg.shape[1]
+    part = width // groups
+    hid_tile = tile_of(hid_width, 256)
+    wide_tile = tile_of(width, 512)
+
+    weight_copies = [
+        pltpu.make_async_copy(src.at[0], dst, w_sem.at[i])
+        for i, (src, dst) in enumerate(((wg_hbm, wg), (wu_hbm, wu), (wd_hbm, wd)))
+    ]
+    for copy in weight_copies:
+        copy.start()
+
+    barrier = pltpu.get_barrier_semaphore()
+    for k in range(1, owners):
+        pl.semaphore_signal(
+            barrier, inc=1, device_id={"expert": lax.rem(me + k, owners)}, device_id_type=MESH
+        )
+    for j in range(1, groups):
+        pl.semaphore_signal(
+            barrier, inc=1, device_id={"dp": lax.rem(grp + j, groups)}, device_id_type=MESH
+        )
+
+    expert_no = lax.broadcasted_iota(jnp.int32, (owners, tok_count), 0)
+    first = ids_ref[0:1, :] == expert_no
+    second = ids_ref[1:2, :] == expert_no
+    named = jnp.where(first, 1.0, 0.0) + jnp.where(second, 1.0, 0.0)
+    gate_of = jnp.where(first, gates_ref[0:1, :], 0.0) + jnp.where(second, gates_ref[1:2, :], 0.0)
+    earlier = jnp.where(
+        lax.broadcasted_iota(jnp.int32, (tok_count, tok_count), 0)
+        < lax.broadcasted_iota(jnp.int32, (tok_count, tok_count), 1),
+        1.0, 0.0,
+    ).astype(BF16)
+    position = jnp.dot(named.astype(BF16), earlier, preferred_element_type=F32)
+    position = jnp.where(named > 0.5, position, -1.0)
+    slot_no = lax.broadcasted_iota(jnp.int32, (capacity, tok_count), 0).astype(F32)
+    for e in range(owners):
+        chosen = jnp.where(slot_no == position[e:e + 1, :], 1.0, 0.0)
+        pick[e * capacity:(e + 1) * capacity, :] = chosen.astype(BF16)
+        gate_col[e * capacity:(e + 1) * capacity, :] = jnp.broadcast_to(
+            jnp.sum(chosen * gate_of[e:e + 1, :], axis=1, keepdims=True), (capacity, 128)
+        )
+
+    @pl.loop(0, width // wide_tile)
+    def _(n):
+        cols = pl.ds(pl.multiple_of(n * wide_tile, wide_tile), wide_tile)
+        picked = jnp.dot(pick[...], tok_ref[:, cols], preferred_element_type=F32)
+        send_tok[:, :, cols] = picked.astype(BF16).reshape(owners, capacity, wide_tile)
+
+    pl.semaphore_wait(barrier, owners - 1 + groups - 1)
+
+    def across(src, dst, send, recv, k):
+        return pltpu.make_async_remote_copy(
+            src_ref=src, dst_ref=dst, send_sem=send, recv_sem=recv,
+            device_id={"expert": lax.rem(me + k, owners)}, device_id_type=MESH,
+        )
+
+    def aside(src, dst, send, recv, j):
+        return pltpu.make_async_remote_copy(
+            src_ref=src, dst_ref=dst, send_sem=send, recv_sem=recv,
+            device_id={"dp": lax.rem(grp + j, groups)}, device_id_type=MESH,
+        )
+
+    def send_block(sent, held, send, recv, k):
+        return across(sent.at[lax.rem(me + k, owners)], held.at[me], send.at[k], recv.at[k], k)
+
+    def take_block(sent, held, send, recv, k):
+        source = lax.rem(me + owners - k, owners)
+        across(sent.at[source], held.at[source], send.at[k], recv.at[k], k).wait_recv()
+        return source
+
+    def share(held, parts, send, recv, k, j):
+        source = lax.rem(me + owners - k, owners)
+        target = lax.rem(grp + j, groups)
+        cols = pl.ds(pl.multiple_of(target * part, part), part)
+        return aside(
+            held.at[source, :, cols], parts.at[grp, source], send.at[k, j], recv.at[k, j], j
+        )
+
+    def take_share(held, parts, send, recv, k, j):
+        source = lax.rem(me + owners - k, owners)
+        origin = lax.rem(grp + groups - j, groups)
+        aside(
+            held.at[source, :, pl.ds(0, part)], parts.at[origin, source],
+            send.at[k, j], recv.at[k, j], j,
+        ).wait_recv()
+
+    def spread(held, send, recv, j):
+        return aside(held.at[grp], held.at[grp], send.at[j], recv.at[j], j)
+
+    def take_spread(held, send, recv, j):
+        origin = lax.rem(grp + groups - j, groups)
+        aside(held.at[origin], held.at[origin], send.at[j], recv.at[j], j).wait_recv()
+        return origin
+
+    for k in range(1, owners):
+        send_block(send_tok, rows, tok_s, tok_r, k).start()
+
+    @pl.loop(0, width // wide_tile)
+    def _(n):
+        cols = pl.ds(pl.multiple_of(n * wide_tile, wide_tile), wide_tile)
+        picked = jnp.dot(pick[...], cot_ref[:, cols], preferred_element_type=F32)
+        picked = picked * gate_col[:, 0:1]
+        send_cot[:, :, cols] = picked.astype(BF16).reshape(owners, capacity, wide_tile)
+
+    rows[me] = send_tok[me]
+    scaled[me] = send_cot[me]
+    for j in range(1, groups):
+        share(rows, x_rows, fr_s, fr_r, 0, j).start()
+    for k in range(1, owners):
+        take_block(send_tok, rows, tok_s, tok_r, k)
+        for j in range(1, groups):
+            share(rows, x_rows, fr_s, fr_r, k, j).start()
+        send_block(send_tok, rows, tok_s, tok_r, k).wait_send()
+        send_block(send_cot, scaled, cot_s, cot_r, k).start()
+
+    mine = pl.ds(pl.multiple_of(grp * part, part), part)
+    own_rows = pltpu.make_async_copy(rows.at[:, :, mine], x_rows.at[grp], own_sem.at[0])
+    own_rows.start()
+    weight_copies[0].wait()
+    weight_copies[1].wait()
+
+    @pl.loop(0, hid_width // hid_tile)
+    def _(n):
+        cols = pl.ds(pl.multiple_of(n * hid_tile, hid_tile), hid_tile)
+        held = rows[...].reshape(slots, width)
+        gate = jnp.dot(held, wg[:, cols], preferred_element_type=F32)
+        up = jnp.dot(held, wu[:, cols], preferred_element_type=F32)
+        pre_gate[:, cols] = gate
+        pre_up[:, cols] = up
+        x_hid[grp, :, cols] = (gate * jax.nn.sigmoid(gate) * up).astype(BF16)
+
+    for j in range(1, groups):
+        spread(x_hid, h_s, h_r, j).start()
+    for j in range(1, groups):
+        share(scaled, x_scaled, fc_s, fc_r, 0, j).start()
+    for k in range(1, owners):
+        take_block(send_cot, scaled, cot_s, cot_r, k)
+        for j in range(1, groups):
+            share(scaled, x_scaled, fc_s, fc_r, k, j).start()
+    own_scaled = pltpu.make_async_copy(scaled.at[:, :, mine], x_scaled.at[grp], own_sem.at[1])
+    own_scaled.start()
+    weight_copies[2].wait()
+    score[...] = jnp.zeros_like(score)
+
+    @pl.loop(0, hid_width // hid_tile)
+    def _(n):
+        cols = pl.ds(pl.multiple_of(n * hid_tile, hid_tile), hid_tile)
+        grad_hidden = dot_nt(scaled[...].reshape(slots, width), wd[cols, :])
+        gate = pre_gate[:, cols]
+        sig = jax.nn.sigmoid(gate)
+        x_gg[grp, :, cols] = (
+            grad_hidden * pre_up[:, cols] * sig * (1.0 + gate * (1.0 - sig))
+        ).astype(BF16)
+        x_gu[grp, :, cols] = (grad_hidden * (gate * sig)).astype(BF16)
+        score[...] += jnp.broadcast_to(
+            jnp.sum(x_hid[grp, :, cols].astype(F32) * grad_hidden, axis=1, keepdims=True),
+            (slots, 128),
+        )
+
+    for j in range(1, groups):
+        spread(x_gg, gg_s, gg_r, j).start()
+        spread(x_gu, gu_s, gu_r, j).start()
+
+    @pl.loop(0, width // wide_tile)
+    def _(n):
+        cols = pl.ds(pl.multiple_of(n * wide_tile, wide_tile), wide_tile)
+        grad = dot_nt(x_gg[grp], wg[cols, :]) + dot_nt(x_gu[grp], wu[cols, :])
+        back_send[:, :, cols] = grad.astype(BF16).reshape(owners, capacity, wide_tile)
+
+    on_diagonal = lax.broadcasted_iota(jnp.int32, (capacity, 128), 0) == lax.broadcasted_iota(
+        jnp.int32, (capacity, 128), 1
+    )
+    for e in range(owners):
+        line = jnp.sum(
+            jnp.where(on_diagonal, score[e * capacity:(e + 1) * capacity, :], 0.0),
+            axis=0, keepdims=True,
+        )
+        score_send[e] = jnp.broadcast_to(line, (8, 128))
+    for k in range(1, owners):
+        send_block(back_send, back_recv, back_s, back_r, k).start()
+        send_block(score_send, score_recv, sc_s, sc_r, k).start()
+    back_recv[me] = back_send[me]
+    score_recv[me] = score_send[me]
+
+    own_rows.wait()
+    own_scaled.wait()
+    for j in range(1, groups):
+        take_spread(x_hid, h_s, h_r, j)
+        for k in range(owners):
+            take_share(rows, x_rows, fr_s, fr_r, k, j)
+            take_share(scaled, x_scaled, fc_s, fc_r, k, j)
+
+    @pl.loop(0, hid_width // hid_tile)
+    def _(n):
+        cols = pl.ds(pl.multiple_of(n * hid_tile, hid_tile), hid_tile)
+        gwd_ref[cols, :] = dot_tn(
+            x_hid[:, :, cols].reshape(groups * slots, hid_tile),
+            x_scaled[...].reshape(groups * slots, part),
+        ).astype(BF16)
+
+    def add_group(origin, begin, end):
+        @pl.loop(0, hid_width // hid_tile)
+        def _(n):
+            cols = pl.ds(pl.multiple_of(n * hid_tile, hid_tile), hid_tile)
+            left = x_rows[origin].reshape(slots, part)
+            gate = dot_tn(left, x_gg[origin, :, cols])
+            up = dot_tn(left, x_gu[origin, :, cols])
+            if not begin:
+                gate = gate + acc_gate[:, cols]
+                up = up + acc_up[:, cols]
+            if end:
+                gwg_ref[:, cols] = gate.astype(BF16)
+                gwu_ref[:, cols] = up.astype(BF16)
+            else:
+                acc_gate[:, cols] = gate
+                acc_up[:, cols] = up
+
+    add_group(grp, True, groups == 1)
+
+    for k in range(1, owners):
+        take_block(back_send, back_recv, back_s, back_r, k)
+        take_block(score_send, score_recv, sc_s, sc_r, k)
+
+    @pl.loop(0, width // wide_tile)
+    def _(n):
+        cols = pl.ds(pl.multiple_of(n * wide_tile, wide_tile), wide_tile)
+        gtok_ref[:, cols] = dot_tn(
+            pick[...], back_recv[:, :, cols].reshape(slots, wide_tile)
+        ).astype(BF16)
+
+    first_sum = jnp.zeros((1, tok_count), F32)
+    second_sum = jnp.zeros((1, tok_count), F32)
+    for e in range(owners):
+        column = jnp.sum(
+            jnp.where(on_diagonal, jnp.broadcast_to(score_recv[e, 0:1, :], (capacity, 128)), 0.0),
+            axis=1, keepdims=True,
+        )
+        by_token = jnp.sum(
+            pick[e * capacity:(e + 1) * capacity, :].astype(F32) * column, axis=0, keepdims=True
+        )
+        first_sum = first_sum + jnp.where(ids_ref[0:1, :] == e, by_token, 0.0)
+        second_sum = second_sum + jnp.where(ids_ref[1:2, :] == e, by_token, 0.0)
+    ggate_ref[0:1, :] = first_sum / gates_ref[0:1, :]
+    ggate_ref[1:2, :] = second_sum / gates_ref[1:2, :]
+
+    for j in range(1, groups):
+        origin = take_spread(x_gg, gg_s, gg_r, j)
+        take_spread(x_gu, gu_s, gu_r, j)
+        add_group(origin, False, j == groups - 1)
+
+    for k in range(1, owners):
+        send_block(send_cot, scaled, cot_s, cot_r, k).wait_send()
+        send_block(back_send, back_recv, back_s, back_r, k).wait_send()
+        send_block(score_send, score_recv, sc_s, sc_r, k).wait_send()
+    for j in range(1, groups):
+        spread(x_hid, h_s, h_r, j).wait_send()
+        spread(x_gg, gg_s, gg_r, j).wait_send()
+        spread(x_gu, gu_s, gu_r, j).wait_send()
+        for k in range(owners):
+            share(rows, x_rows, fr_s, fr_r, k, j).wait_send()
+            share(scaled, x_scaled, fc_s, fc_r, k, j).wait_send()
+
+
+def kernel_body(tokens, expert_ids, gates, cotangent, w_gate, w_up, w_down):
+    tok_rows, width = tokens.shape
+    owners = lax.axis_size("expert")
+    groups = lax.axis_size("dp")
+    capacity = slots_of(tok_rows, expert_ids.shape[1], owners)
+    hid_width = w_gate.shape[2]
+    part = width // groups
+    slots = owners * capacity
+    vmem = pl.BlockSpec(memory_space=pltpu.VMEM)
+    dma = pltpu.SemaphoreType.DMA
+    blocks = pltpu.VMEM((owners, capacity, width), BF16)
+    parts = pltpu.VMEM((groups, owners, capacity, part), BF16)
+    hids = pltpu.VMEM((groups, slots, hid_width), BF16)
+    lines = pltpu.VMEM((owners, 8, 128), F32)
+    per_owner, per_group, per_share = dma((owners,)), dma((groups,)), dma((owners, groups))
+    grad_tokens, grad_gates, grad_gate, grad_up, grad_down = pl.pallas_call(
+        functools.partial(layer_kernel, owners, groups, capacity),
+        out_shape=(
+            jax.ShapeDtypeStruct((tok_rows, width), BF16),
+            jax.ShapeDtypeStruct((2, tok_rows), F32),
+            jax.ShapeDtypeStruct((part, hid_width), BF16),
+            jax.ShapeDtypeStruct((part, hid_width), BF16),
+            jax.ShapeDtypeStruct((hid_width, part), BF16),
+        ),
+        in_specs=[vmem] * 4 + [pl.BlockSpec(memory_space=pl.ANY)] * 3,
+        out_specs=(vmem,) * 5,
+        scratch_shapes=[
+            pltpu.VMEM((width, hid_width), BF16),
+            pltpu.VMEM((width, hid_width), BF16),
+            pltpu.VMEM((hid_width, width), BF16),
+            dma((3,)),
+            pltpu.VMEM((slots, tok_rows), BF16),
+            pltpu.VMEM((slots, 128), F32),
+            blocks, blocks, blocks, blocks,
+            pltpu.VMEM((slots, hid_width), F32),
+            pltpu.VMEM((slots, hid_width), F32),
+            pltpu.VMEM((slots, 128), F32),
+            parts, parts, hids, hids, hids,
+            dma((2,)),
+            blocks, blocks, lines, lines,
+            pltpu.VMEM((part, hid_width), F32),
+            pltpu.VMEM((part, hid_width), F32),
+        ]
+        + [per_owner] * 8 + [per_share] * 4 + [per_group] * 6,
+        compiler_params=pltpu.CompilerParams(
+            collective_id=0, has_side_effects=True, vmem_limit_bytes=56 * 1024 * 1024
+        ),
+        cost_estimate=pl.CostEstimate(
+            flops=16 * slots * width * hid_width,
+            bytes_accessed=6 * width * hid_width * 2,
+            transcendentals=2 * slots * hid_width,
+        ),
+        name="expert_layer",
+    )(
+        expert_ids.T, gates.astype(F32).T, tokens, cotangent, w_gate, w_up, w_down
+    )
+    return (grad_tokens, grad_gates.T.astype(BF16), grad_gate[None], grad_up[None], grad_down[None])
 
 
 def contract_rows(left, right):
@@ -61,7 +421,7 @@
     return (back_rows, back_scores)
 
 
-def body(tokens, expert_ids, gates, cotangent, w_gate, w_up, w_down):
+def plain_body(tokens, expert_ids, gates, cotangent, w_gate, w_up, w_down):
     tok_rows, model_width = tokens.shape
     top_count = expert_ids.shape[1]
     owners = lax.axis_size("expert")
@@ -112,6 +472,16 @@
     return (grad_tokens, grad_gates, grad_w_gate, grad_w_up, grad_w_down)
 
 
+def slots_of(tok_rows, top_count, owners):
+    return min(tok_rows, 3 * tok_rows * top_count // (2 * owners))
+
+
+def body(tokens, expert_ids, gates, cotangent, w_gate, w_up, w_down):
+    capacity = slots_of(tokens.shape[0], expert_ids.shape[1], lax.axis_size("expert"))
+    chosen = kernel_body if capacity % 16 == 0 else plain_body
+    return chosen(tokens, expert_ids, gates, cotangent, w_gate, w_up, w_down)
+
+
 def solution(mesh):
     placed = (
         P(("dp", "expert"), None),

time: 272 us -> 168 us (0.62)
  the two profiles are of different devices: /device:TPU:0 before, /device:TPU:9 now
where the time goes in v1:
time: 168 us
  Pallas kernels  159 us (95%)
  local copies, waits for them, and re-layouts  5.71 us (3%)
  other arithmetic  2.51 us (1%)
    pallas_call x1, Pallas kernels, kernel_body(): pl.pallas_call(functools.partial(layer_kernel, owners, groups, capacity),...  159 us
    unnamed x8, local copies, waits for them, and re-layouts  5.71 us

profile of v1, /device:TPU:9, one launch (start us, length us, event | category | flops | bytes accessed | tf_op | source)
XLA Modules:
  0.0 168.1 jit_solution(18423944010486966919)
XLA Ops:
  0.6 1.2 convert_bitcast_fusion.gates_ref
  1.9 159.3 %expert_layer.1 = (bf16[128,2048]{1,0:T(8,128)(2,1)}, f32[2,128]{1,0:T(2,128)}, bf16[512,768]{1,0:T(8,128)(2,1)}, bf16[512,768]{1,0:T(8,128)(2,1)}, bf16[768,512]{1,0:T(8,128)(2,1)}) custom-call(s32[2,128]{1,0:T(2,128)} %bitcast.11, f32[2,128]{1,0:T(2,128)} %convert_bitcast_fusion.gates_ref, bf16[128,2048]{1,0:T(8,128)(2,1)} %tok_ref.1, ...), custom_call_target="tpu_custom_call" | custom-call | flops 9663676416 | bytes 18874368 | tf_op jit(solution)/shard_map/expert_layer/pallas_call | solution.py:323
  161.1 0.0 copy-start.1
  161.1 0.0 copy-start
  161.1 1.3 convert_bitcast_fusion.1
  162.4 1.9 %copy.16 = bf16[128,2048]{1,0:T(8,128)(2,1)} copy(bf16[128,2048]{1,0:T(8,128)(2,1)} %get-tuple-element.20) | data formatting | bytes 1048576
  164.3 2.1 %copy.17 = bf16[1,512,768]{2,1,0:T(8,128)(2,1)} copy(bf16[1,512,768]{2,1,0:T(8,128)(2,1)} %bitcast.10) | data formatting | bytes 1572864
  166.4 0.0 copy-done.1
  166.4 0.9 copy.18
  167.3 0.0 copy-done
  167.3 0.9 copy.19
Async XLA Ops:
  161.1 5.3 %copy-start.1 = (bf16[512,768]{1,0:T(8,128)(2,1)S(1)}, bf16[512,768]{1,0:T(8,128)(2,1)}, u32[]{:S(2)}) copy-start(bf16[512,768]{1,0:T(8,128)(2,1)} %get-tuple-element.13) | copy-start | bytes 2359300
  161.1 6.1 %copy-start = (bf16[768,512]{1,0:T(8,128)(2,1)S(1)}, bf16[768,512]{1,0:T(8,128)(2,1)}, u32[]{:S(2)}) copy-start(bf16[768,512]{1,0:T(8,128)(2,1)} %get-tuple-element.14) | copy-start | bytes 2359300

commit v2 on v1

--- a/solution.py
+++ b/solution.py
@@ -17,6 +17,14 @@
     while size % step:
         step -= 128
     return step
+
+
+def paired(index, step, count):
+    total, digit = 0, 1
+    while digit < count:
+        total = total + digit * lax.rem(lax.div(index, digit) + step // digit, 2)
+        digit *= 2
+    return total
 
 
 def dot_nt(left, right):
@@ -57,11 +65,11 @@
     barrier = pltpu.get_barrier_semaphore()
     for k in range(1, owners):
         pl.semaphore_signal(
-            barrier, inc=1, device_id={"expert": lax.rem(me + k, owners)}, device_id_type=MESH
+            barrier, inc=1, device_id={"expert": paired(me, k, owners)}, device_id_type=MESH
         )
     for j in range(1, groups):
         pl.semaphore_signal(
-            barrier, inc=1, device_id={"dp": lax.rem(grp + j, groups)}, device_id_type=MESH
+            barrier, inc=1, device_id={"dp": paired(grp, j, groups)}, device_id_type=MESH
         )
 
     expert_no = lax.broadcasted_iota(jnp.int32, (owners, tok_count), 0)
@@ -95,34 +103,34 @@
     def across(src, dst, send, recv, k):
         return pltpu.make_async_remote_copy(
             src_ref=src, dst_ref=dst, send_sem=send, recv_sem=recv,
-            device_id={"expert": lax.rem(me + k, owners)}, device_id_type=MESH,
+            device_id={"expert": paired(me, k, owners)}, device_id_type=MESH,
         )
 
     def aside(src, dst, send, recv, j):
         return pltpu.make_async_remote_copy(
             src_ref=src, dst_ref=dst, send_sem=send, recv_sem=recv,
-            device_id={"dp": lax.rem(grp + j, groups)}, device_id_type=MESH,
+            device_id={"dp": paired(grp, j, groups)}, device_id_type=MESH,
         )
 
     def send_block(sent, held, send, recv, k):
-        return across(sent.at[lax.rem(me + k, owners)], held.at[me], send.at[k], recv.at[k], k)
+        return across(sent.at[paired(me, k, owners)], held.at[me], send.at[k], recv.at[k], k)
 
     def take_block(sent, held, send, recv, k):
-        source = lax.rem(me + owners - k, owners)
+        source = paired(me, k, owners)
         across(sent.at[source], held.at[source], send.at[k], recv.at[k], k).wait_recv()
         return source
 
     def share(held, parts, send, recv, k, j):
-        source = lax.rem(me + owners - k, owners)
-        target = lax.rem(grp + j, groups)
+        source = paired(me, k, owners)
+        target = paired(grp, j, groups)
         cols = pl.ds(pl.multiple_of(target * part, part), part)
         return aside(
             held.at[source, :, cols], parts.at[grp, source], send.at[k, j], recv.at[k, j], j
         )
 
     def take_share(held, parts, send, recv, k, j):
-        source = lax.rem(me + owners - k, owners)
-        origin = lax.rem(grp + groups - j, groups)
+        source = paired(me, k, owners)
+        origin = paired(grp, j, groups)
         aside(
             held.at[source, :, pl.ds(0, part)], parts.at[origin, source],
             send.at[k, j], recv.at[k, j], j,
@@ -132,11 +140,24 @@
         return aside(held.at[grp], held.at[grp], send.at[j], recv.at[j], j)
 
     def take_spread(held, send, recv, j):
-        origin = lax.rem(grp + groups - j, groups)
+        origin = paired(grp, j, groups)
         aside(held.at[origin], held.at[origin], send.at[j], recv.at[j], j).wait_recv()
         return origin
 
-    for k in range(1, owners):
+    def hand_on(held, send, recv, j):
+        half = slots // 2
+        source = paired(grp, j, groups)
+        lines = pl.ds((j - 1) * half, half)
+        block = held.at[source, lines]
+        return aside(block, block, send.at[3 * (2 - j)], recv.at[3 * (2 - j)], 3 - j)
+
+    def take_on(held, send, recv, j):
+        half = slots // 2
+        block = held.at[paired(grp, 3, groups), pl.ds((j - 1) * half, half)]
+        aside(block, block, send.at[3 * (2 - j)], recv.at[3 * (2 - j)], 3 - j).wait_recv()
+
+    far_first = range(owners - 1, 0, -1)
+    for k in far_first:
         send_block(send_tok, rows, tok_s, tok_r, k).start()
 
     @pl.loop(0, width // wide_tile)
@@ -150,12 +171,12 @@
     scaled[me] = send_cot[me]
     for j in range(1, groups):
         share(rows, x_rows, fr_s, fr_r, 0, j).start()
-    for k in range(1, owners):
+    for k in far_first:
+        send_block(send_tok, rows, tok_s, tok_r, k).wait_send()
+        send_block(send_cot, scaled, cot_s, cot_r, k).start()
         take_block(send_tok, rows, tok_s, tok_r, k)
         for j in range(1, groups):
             share(rows, x_rows, fr_s, fr_r, k, j).start()
-        send_block(send_tok, rows, tok_s, tok_r, k).wait_send()
-        send_block(send_cot, scaled, cot_s, cot_r, k).start()
 
     mine = pl.ds(pl.multiple_of(grp * part, part), part)
     own_rows = pltpu.make_async_copy(rows.at[:, :, mine], x_rows.at[grp], own_sem.at[0])
@@ -173,14 +194,18 @@
         pre_up[:, cols] = up
         x_hid[grp, :, cols] = (gate * jax.nn.sigmoid(gate) * up).astype(BF16)
 
-    for j in range(1, groups):
+    for j in (1, 2):
         spread(x_hid, h_s, h_r, j).start()
     for j in range(1, groups):
         share(scaled, x_scaled, fc_s, fc_r, 0, j).start()
-    for k in range(1, owners):
+    for k in far_first:
         take_block(send_cot, scaled, cot_s, cot_r, k)
         for j in range(1, groups):
             share(scaled, x_scaled, fc_s, fc_r, k, j).start()
+        if k == owners // 2:
+            for j in (1, 2):
+                take_spread(x_hid, h_s, h_r, j)
+                hand_on(x_hid, h_s, h_r, j).start()
     own_scaled = pltpu.make_async_copy(scaled.at[:, :, mine], x_scaled.at[grp], own_sem.at[1])
     own_scaled.start()
     weight_copies[2].wait()
@@ -201,8 +226,9 @@
             (slots, 128),
         )
 
-    for j in range(1, groups):
+    for j in (1, 2):
         spread(x_gg, gg_s, gg_r, j).start()
+    for j in (1, 2):
         spread(x_gu, gu_s, gu_r, j).start()
 
     @pl.loop(0, width // wide_tile)
@@ -220,7 +246,7 @@
             axis=0, keepdims=True,
         )
         score_send[e] = jnp.broadcast_to(line, (8, 128))
-    for k in range(1, owners):
+    for k in far_first:
         send_block(back_send, back_recv, back_s, back_r, k).start()
         send_block(score_send, score_recv, sc_s, sc_r, k).start()
     back_recv[me] = back_send[me]
@@ -228,8 +254,9 @@
 
     own_rows.wait()
     own_scaled.wait()
+    for j in (1, 2):
+        take_on(x_hid, h_s, h_r, j)
     for j in range(1, groups):
-        take_spread(x_hid, h_s, h_r, j)
         for k in range(owners):
             take_share(rows, x_rows, fr_s, fr_r, k, j)
             take_share(scaled, x_scaled, fc_s, fc_r, k, j)
@@ -259,7 +286,14 @@
                 acc_gate[:, cols] = gate
                 acc_up[:, cols] = up
 
-    add_group(grp, True, groups == 1)
+    add_group(grp, True, False)
+    for j in (1, 2):
+        take_spread(x_gg, gg_s, gg_r, j)
+        hand_on(x_gg, gg_s, gg_r, j).start()
+    for j in (1, 2):
+        origin = take_spread(x_gu, gu_s, gu_r, j)
+        hand_on(x_gu, gu_s, gu_r, j).start()
+        add_group(origin, False, False)
 
     for k in range(1, owners):
         take_block(back_send, back_recv, back_s, back_r, k)
@@ -287,22 +321,34 @@
     ggate_ref[0:1, :] = first_sum / gates_ref[0:1, :]
     ggate_ref[1:2, :] = second_sum / gates_ref[1:2, :]
 
-    for j in range(1, groups):
-        origin = take_spread(x_gg, gg_s, gg_r, j)
-        take_spread(x_gu, gu_s, gu_r, j)
-        add_group(origin, False, j == groups - 1)
+    for j in (1, 2):
+        take_on(x_gg, gg_s, gg_r, j)
+        take_on(x_gu, gu_s, gu_r, j)
+    add_group(paired(grp, 3, groups), False, True)
 
     for k in range(1, owners):
         send_block(send_cot, scaled, cot_s, cot_r, k).wait_send()
         send_block(back_send, back_recv, back_s, back_r, k).wait_send()
         send_block(score_send, score_recv, sc_s, sc_r, k).wait_send()
+    for j in (1, 2):
+        for held, send, recv in ((x_hid, h_s, h_r), (x_gg, gg_s, gg_r), (x_gu, gu_s, gu_r)):
+            spread(held, send, recv, j).wait_send()
+            hand_on(held, send, recv, j).wait_send()
     for j in range(1, groups):
-        spread(x_hid, h_s, h_r, j).wait_send()
-        spread(x_gg, gg_s, gg_r, j).wait_send()
-        spread(x_gu, gu_s, gu_r, j).wait_send()
         for k in range(owners):
             share(rows, x_rows, fr_s, fr_r, k, j).wait_send()
             share(scaled, x_scaled, fc_s, fc_r, k, j).wait_send()
+
+
+def hand_over(*refs):
+    count = (len(refs) - 1) // 2
+    copies = [
+        pltpu.make_async_copy(refs[i], refs[count + i], refs[-1].at[i]) for i in range(count)
+    ]
+    for copy in copies:
+        copy.start()
+    for copy in copies:
+        copy.wait()
 
 
 def kernel_body(tokens, expert_ids, gates, cotangent, w_gate, w_up, w_down):
@@ -361,7 +407,17 @@
     )(
         expert_ids.T, gates.astype(F32).T, tokens, cotangent, w_gate, w_up, w_down
     )
-    return (grad_tokens, grad_gates.T.astype(BF16), grad_gate[None], grad_up[None], grad_down[None])
+    held = (grad_tokens, grad_gate[None], grad_up[None], grad_down[None])
+    anywhere = pl.BlockSpec(memory_space=pl.ANY)
+    grad_tokens, grad_gate, grad_up, grad_down = pl.pallas_call(
+        hand_over,
+        out_shape=tuple(jax.ShapeDtypeStruct(x.shape, x.dtype) for x in held),
+        in_specs=[anywhere] * len(held),
+        out_specs=(anywhere,) * len(held),
+        scratch_shapes=[dma((len(held),))],
+        name="hand_over",
+    )(*held)
+    return (grad_tokens, grad_gates.T.astype(BF16), grad_gate, grad_up, grad_down)
 
 
 def contract_rows(left, right):
@@ -478,7 +534,8 @@
 
 def body(tokens, expert_ids, gates, cotangent, w_gate, w_up, w_down):
     capacity = slots_of(tokens.shape[0], expert_ids.shape[1], lax.axis_size("expert"))
-    chosen = kernel_body if capacity % 16 == 0 else plain_body
+    even = lax.axis_size("dp") == 4 and lax.axis_size("expert") == 8
+    chosen = kernel_body if even and capacity % 16 == 0 else plain_body
     return chosen(tokens, expert_ids, gates, cotangent, w_gate, w_up, w_down)
 
 

time: 168 us -> 239 us (1.42)
  the two profiles are of different devices: /device:TPU:9 before, /device:TPU:0 now
where the time goes in v2:
time: 239 us
  Pallas kernels  236 us (99%)
  other arithmetic  2.39 us (1%)
    pallas_call x1, Pallas kernels, kernel_body(): pl.pallas_call(functools.partial(layer_kernel, owners, groups, capacity),...  148 us
    pallas_call x1, Pallas kernels, kernel_body(): pl.pallas_call(hand_over, out_shape=tuple((jax.ShapeDtypeStruct(x.shape,...  88.5 us

profile of v2, /device:TPU:0, one launch (start us, length us, event | category | flops | bytes accessed | tf_op | source)
XLA Modules:
  0.0 239.2 jit_solution(14920827474758948258)
XLA Ops:
  0.6 1.2 convert_bitcast_fusion.gates_ref
  1.9 147.7 %expert_layer.1 = (bf16[128,2048]{1,0:T(8,128)(2,1)}, f32[2,128]{1,0:T(2,128)}, bf16[512,768]{1,0:T(8,128)(2,1)}, bf16[512,768]{1,0:T(8,128)(2,1)}, bf16[768,512]{1,0:T(8,128)(2,1)}) custom-call(s32[2,128]{1,0:T(2,128)} %bitcast.11, f32[2,128]{1,0:T(2,128)} %convert_bitcast_fusion.gates_ref, bf16[128,2048]{1,0:T(8,128)(2,1)} %tok_ref.1, ...), custom_call_target="tpu_custom_call" | custom-call | flops 9663676416 | bytes 18874368 | tf_op jit(solution)/shard_map/expert_layer/pallas_call | solution.py:369
  149.5 88.5 %hand_over.1 = (bf16[128,2048]{1,0:T(8,128)(2,1)}, bf16[1,512,768]{2,1,0:T(8,128)(2,1)}, bf16[1,512,768]{2,1,0:T(8,128)(2,1)}, bf16[1,768,512]{2,1,0:T(8,128)(2,1)}) custom-call(bf16[128,2048]{1,0:T(8,128)(2,1)} %get-tuple-element.14.refs_0_, bf16[1,512,768]{2,1,0:T(8,128)(2,1)} %bitcast.8, bf16[1,512,768]{2,1,0:T(8,128)(2,1)} %bitcast.9, ...), custom_call_target="tpu_custom_call" | custom-call | tf_op jit(solution)/shard_map/hand_over/pallas_call | solution.py:412
  238.0 1.2 convert_bitcast_fusion.1

commit v3 on v2

--- a/solution.py
+++ b/solution.py
@@ -22,7 +22,7 @@
 def paired(index, step, count):
     total, digit = 0, 1
     while digit < count:
-        total = total + digit * lax.rem(lax.div(index, digit) + step // digit, 2)
+        total = total + digit * lax.rem(lax.div(index, digit) + lax.div(step, digit), 2)
         digit *= 2
     return total
 
@@ -156,8 +156,14 @@
         block = held.at[paired(grp, 3, groups), pl.ds((j - 1) * half, half)]
         aside(block, block, send.at[3 * (2 - j)], recv.at[3 * (2 - j)], 3 - j).wait_recv()
 
-    far_first = range(owners - 1, 0, -1)
-    for k in far_first:
+    chip = lax.div(me, 2)
+    inner = lax.rem(lax.div(chip + 1, 2), 2)
+    out_order, in_order = [1], [1]
+    for i in range(3):
+        for core in range(2):
+            out_order.append(2 * (1 + lax.rem(i + inner, 3)) + core)
+            in_order.append(2 * (1 + lax.rem(i + 1 - inner, 3)) + core)
+    for k in out_order:
         send_block(send_tok, rows, tok_s, tok_r, k).start()
 
     @pl.loop(0, width // wide_tile)
@@ -171,9 +177,9 @@
     scaled[me] = send_cot[me]
     for j in range(1, groups):
         share(rows, x_rows, fr_s, fr_r, 0, j).start()
-    for k in far_first:
-        send_block(send_tok, rows, tok_s, tok_r, k).wait_send()
-        send_block(send_cot, scaled, cot_s, cot_r, k).start()
+    for out, k in zip(out_order, in_order):
+        send_block(send_tok, rows, tok_s, tok_r, out).wait_send()
+        send_block(send_cot, scaled, cot_s, cot_r, out).start()
         take_block(send_tok, rows, tok_s, tok_r, k)
         for j in range(1, groups):
             share(rows, x_rows, fr_s, fr_r, k, j).start()
@@ -198,11 +204,11 @@
         spread(x_hid, h_s, h_r, j).start()
     for j in range(1, groups):
         share(scaled, x_scaled, fc_s, fc_r, 0, j).start()
-    for k in far_first:
+    for step, k in enumerate(in_order):
         take_block(send_cot, scaled, cot_s, cot_r, k)
         for j in range(1, groups):
             share(scaled, x_scaled, fc_s, fc_r, k, j).start()
-        if k == owners // 2:
+        if step == owners // 2:
             for j in (1, 2):
                 take_spread(x_hid, h_s, h_r, j)
                 hand_on(x_hid, h_s, h_r, j).start()
@@ -246,7 +252,7 @@
             axis=0, keepdims=True,
         )
         score_send[e] = jnp.broadcast_to(line, (8, 128))
-    for k in far_first:
+    for k in out_order:
         send_block(back_send, back_recv, back_s, back_r, k).start()
         send_block(score_send, score_recv, sc_s, sc_r, k).start()
     back_recv[me] = back_send[me]
@@ -341,14 +347,9 @@
 
 
 def hand_over(*refs):
-    count = (len(refs) - 1) // 2
-    copies = [
-        pltpu.make_async_copy(refs[i], refs[count + i], refs[-1].at[i]) for i in range(count)
-    ]
-    for copy in copies:
-        copy.start()
-    for copy in copies:
-        copy.wait()
+    count = len(refs) // 2
+    for i in range(count):
+        refs[count + i][...] = refs[i][...]
 
 
 def kernel_body(tokens, expert_ids, gates, cotangent, w_gate, w_up, w_down):
@@ -408,13 +409,19 @@
         expert_ids.T, gates.astype(F32).T, tokens, cotangent, w_gate, w_up, w_down
     )
     held = (grad_tokens, grad_gate[None], grad_up[None], grad_down[None])
-    anywhere = pl.BlockSpec(memory_space=pl.ANY)
+    quarters = [
+        pl.BlockSpec(
+            x.shape[:-2] + (x.shape[-2] // 4, x.shape[-1]),
+            (lambda n: (n, 0)) if x.ndim == 2 else (lambda n: (0, n, 0)),
+        )
+        for x in held
+    ]
     grad_tokens, grad_gate, grad_up, grad_down = pl.pallas_call(
         hand_over,
+        grid=(4,),
         out_shape=tuple(jax.ShapeDtypeStruct(x.shape, x.dtype) for x in held),
-        in_specs=[anywhere] * len(held),
-        out_specs=(anywhere,) * len(held),
-        scratch_shapes=[dma((len(held),))],
+        in_specs=quarters,
+        out_specs=tuple(quarters),
         name="hand_over",
     )(*held)
     return (grad_tokens, grad_gates.T.astype(BF16), grad_gate, grad_up, grad_down)

time: 239 us -> 137 us (0.57)
  Pallas kernels: 236 us -> 133 us
    pallas_call x1, Pallas kernels: 88.5 us -> 4.14 us  [kernel_body(): pl.pallas_call(hand_over, grid=(4,), out_shape=tuple((jax.ShapeDtypeStruc...]
    pallas_call x1, Pallas kernels: 148 us -> 129 us  [kernel_body(): pl.pallas_call(functools.partial(layer_kernel, owners, groups, capacity),...]
where the time goes in v3:
time: 137 us; the launch traced here: 136 us
  Pallas kernels  133 us (97%)
  other arithmetic  2.39 us (2%)
    pallas_call x1, Pallas kernels, kernel_body(): pl.pallas_call(functools.partial(layer_kernel, owners, groups, capacity),...  129 us
    pallas_call x1, Pallas kernels, kernel_body(): pl.pallas_call(hand_over, grid=(4,), out_shape=tuple((jax.ShapeDtypeStruc...  4.14 us

profile of v3, /device:TPU:0, one launch (start us, length us, event | category | flops | bytes accessed | tf_op | source)
XLA Modules:
  0.0 136.3 jit_solution(6583522363742536443)
XLA Ops:
  0.6 1.2 convert_bitcast_fusion.gates_ref
  1.9 129.1 %expert_layer.1 = (bf16[128,2048]{1,0:T(8,128)(2,1)}, f32[2,128]{1,0:T(2,128)}, bf16[512,768]{1,0:T(8,128)(2,1)}, bf16[512,768]{1,0:T(8,128)(2,1)}, bf16[768,512]{1,0:T(8,128)(2,1)}) custom-call(s32[2,128]{1,0:T(2,128)} %bitcast.11, f32[2,128]{1,0:T(2,128)} %convert_bitcast_fusion.gates_ref, bf16[128,2048]{1,0:T(8,128)(2,1)} %tok_ref.1, ...), custom_call_target="tpu_custom_call" | custom-call | flops 9663676416 | bytes 18874368 | tf_op jit(solution)/shard_map/expert_layer/pallas_call | solution.py:370
  131.0 4.1 %hand_over.1 = (bf16[128,2048]{1,0:T(8,128)(2,1)}, bf16[1,512,768]{2,1,0:T(8,128)(2,1)}, bf16[1,512,768]{2,1,0:T(8,128)(2,1)}, bf16[1,768,512]{2,1,0:T(8,128)(2,1)}) custom-call(bf16[128,2048]{1,0:T(8,128)(2,1)} %get-tuple-element.14.refs_0_, bf16[1,512,768]{2,1,0:T(8,128)(2,1)} %bitcast.8, bf16[1,512,768]{2,1,0:T(8,128)(2,1)} %bitcast.9, ...), custom_call_target="tpu_custom_call" | custom-call | tf_op jit(solution)/shard_map/hand_over/pallas_call | solution.py:419
  135.1 1.2 convert_bitcast_fusion.1

commit v4 on v3

--- a/solution.py
+++ b/solution.py
@@ -40,7 +40,7 @@
     ids_ref, gates_ref, tok_ref, cot_ref, wg_hbm, wu_hbm, wd_hbm,
     gtok_ref, ggate_ref, gwg_ref, gwu_ref, gwd_ref,
     wg, wu, wd, w_sem,
-    pick, gate_col, send_tok, send_cot, rows, scaled, pre_gate, pre_up, score,
+    pick, gate_col, send_tok, send_cot, rows, scaled, gate_factor, up_factor, score,
     x_rows, x_scaled, x_hid, x_gg, x_gu, own_sem,
     back_send, back_recv, score_send, score_recv, acc_gate, acc_up,
     tok_s, tok_r, cot_s, cot_r, back_s, back_r, sc_s, sc_r,
@@ -76,7 +76,8 @@
     first = ids_ref[0:1, :] == expert_no
     second = ids_ref[1:2, :] == expert_no
     named = jnp.where(first, 1.0, 0.0) + jnp.where(second, 1.0, 0.0)
-    gate_of = jnp.where(first, gates_ref[0:1, :], 0.0) + jnp.where(second, gates_ref[1:2, :], 0.0)
+    weights = gates_ref[...].astype(F32)
+    gate_of = jnp.where(first, weights[0:1, :], 0.0) + jnp.where(second, weights[1:2, :], 0.0)
     earlier = jnp.where(
         lax.broadcasted_iota(jnp.int32, (tok_count, tok_count), 0)
         < lax.broadcasted_iota(jnp.int32, (tok_count, tok_count), 1),
@@ -156,6 +157,43 @@
         block = held.at[paired(grp, 3, groups), pl.ds((j - 1) * half, half)]
         aside(block, block, send.at[3 * (2 - j)], recv.at[3 * (2 - j)], 3 - j).wait_recv()
 
+    def tile(n):
+        return pl.ds(pl.multiple_of(n * hid_tile, hid_tile), hid_tile)
+
+    def spread_tile(held, send, recv, n, j):
+        block = held.at[grp, :, tile(n)]
+        return aside(block, block, send.at[n, j], recv.at[n, j], j)
+
+    def take_tile(held, send, recv, n, j):
+        block = held.at[paired(grp, j, groups), :, tile(n)]
+        aside(block, block, send.at[n, j], recv.at[n, j], j).wait_recv()
+
+    def hand_on_tile(held, send, recv, n, j):
+        half = slots // 2
+        block = held.at[paired(grp, j, groups), pl.ds((j - 1) * half, half), tile(n)]
+        return aside(block, block, send.at[n, 3 * (2 - j)], recv.at[n, 3 * (2 - j)], 3 - j)
+
+    def take_on_tile(held, send, recv, n, j):
+        half = slots // 2
+        block = held.at[paired(grp, 3, groups), pl.ds((j - 1) * half, half), tile(n)]
+        aside(block, block, send.at[n, 3 * (2 - j)], recv.at[n, 3 * (2 - j)], 3 - j).wait_recv()
+
+    def wide(n):
+        return pl.ds(pl.multiple_of(n * wide_tile, wide_tile), wide_tile)
+
+    def send_back(n, k):
+        return across(
+            back_send.at[paired(me, k, owners), :, wide(n)], back_recv.at[me, :, wide(n)],
+            back_s.at[n, k], back_r.at[n, k], k,
+        )
+
+    def take_back(n, k):
+        source = paired(me, k, owners)
+        across(
+            back_send.at[source, :, wide(n)], back_recv.at[source, :, wide(n)],
+            back_s.at[n, k], back_r.at[n, k], k,
+        ).wait_recv()
+
     chip = lax.div(me, 2)
     inner = lax.rem(lax.div(chip + 1, 2), 2)
     out_order, in_order = [1], [1]
@@ -196,9 +234,11 @@
         held = rows[...].reshape(slots, width)
         gate = jnp.dot(held, wg[:, cols], preferred_element_type=F32)
         up = jnp.dot(held, wu[:, cols], preferred_element_type=F32)
-        pre_gate[:, cols] = gate
-        pre_up[:, cols] = up
-        x_hid[grp, :, cols] = (gate * jax.nn.sigmoid(gate) * up).astype(BF16)
+        sig = jax.nn.sigmoid(gate)
+        active = gate * sig
+        x_hid[grp, :, cols] = (active * up).astype(BF16)
+        gate_factor[:, cols] = up * sig * (1.0 + gate * (1.0 - sig))
+        up_factor[:, cols] = active
 
     for j in (1, 2):
         spread(x_hid, h_s, h_r, j).start()
@@ -221,27 +261,24 @@
     def _(n):
         cols = pl.ds(pl.multiple_of(n * hid_tile, hid_tile), hid_tile)
         grad_hidden = dot_nt(scaled[...].reshape(slots, width), wd[cols, :])
-        gate = pre_gate[:, cols]
-        sig = jax.nn.sigmoid(gate)
-        x_gg[grp, :, cols] = (
-            grad_hidden * pre_up[:, cols] * sig * (1.0 + gate * (1.0 - sig))
-        ).astype(BF16)
-        x_gu[grp, :, cols] = (grad_hidden * (gate * sig)).astype(BF16)
+        x_gg[grp, :, cols] = (grad_hidden * gate_factor[:, cols]).astype(BF16)
+        x_gu[grp, :, cols] = (grad_hidden * up_factor[:, cols]).astype(BF16)
+        for j in (1, 2):
+            spread_tile(x_gg, gg_s, gg_r, n, j).start()
+            spread_tile(x_gu, gu_s, gu_r, n, j).start()
         score[...] += jnp.broadcast_to(
             jnp.sum(x_hid[grp, :, cols].astype(F32) * grad_hidden, axis=1, keepdims=True),
             (slots, 128),
         )
 
-    for j in (1, 2):
-        spread(x_gg, gg_s, gg_r, j).start()
-    for j in (1, 2):
-        spread(x_gu, gu_s, gu_r, j).start()
-
     @pl.loop(0, width // wide_tile)
     def _(n):
         cols = pl.ds(pl.multiple_of(n * wide_tile, wide_tile), wide_tile)
         grad = dot_nt(x_gg[grp], wg[cols, :]) + dot_nt(x_gu[grp], wu[cols, :])
         back_send[:, :, cols] = grad.astype(BF16).reshape(owners, capacity, wide_tile)
+        for k in out_order:
+            send_back(n, k).start()
+        back_recv[me, :, cols] = back_send[me, :, cols]
 
     on_diagonal = lax.broadcasted_iota(jnp.int32, (capacity, 128), 0) == lax.broadcasted_iota(
         jnp.int32, (capacity, 128), 1
@@ -253,9 +290,7 @@
         )
         score_send[e] = jnp.broadcast_to(line, (8, 128))
     for k in out_order:
-        send_block(back_send, back_recv, back_s, back_r, k).start()
         send_block(score_send, score_recv, sc_s, sc_r, k).start()
-    back_recv[me] = back_send[me]
     score_recv[me] = score_send[me]
 
     own_rows.wait()
@@ -275,43 +310,47 @@
             x_scaled[...].reshape(groups * slots, part),
         ).astype(BF16)
 
-    def add_group(origin, begin, end):
-        @pl.loop(0, hid_width // hid_tile)
-        def _(n):
-            cols = pl.ds(pl.multiple_of(n * hid_tile, hid_tile), hid_tile)
-            left = x_rows[origin].reshape(slots, part)
-            gate = dot_tn(left, x_gg[origin, :, cols])
-            up = dot_tn(left, x_gu[origin, :, cols])
-            if not begin:
-                gate = gate + acc_gate[:, cols]
-                up = up + acc_up[:, cols]
-            if end:
-                gwg_ref[:, cols] = gate.astype(BF16)
-                gwu_ref[:, cols] = up.astype(BF16)
-            else:
-                acc_gate[:, cols] = gate
-                acc_up[:, cols] = up
-
-    add_group(grp, True, False)
-    for j in (1, 2):
-        take_spread(x_gg, gg_s, gg_r, j)
-        hand_on(x_gg, gg_s, gg_r, j).start()
-    for j in (1, 2):
-        origin = take_spread(x_gu, gu_s, gu_r, j)
-        hand_on(x_gu, gu_s, gu_r, j).start()
-        add_group(origin, False, False)
+    def terms(origin, cols):
+        left = x_rows[origin].reshape(slots, part)
+        return dot_tn(left, x_gg[origin, :, cols]), dot_tn(left, x_gu[origin, :, cols])
+
+    @pl.loop(0, hid_width // hid_tile)
+    def _(n):
+        acc_gate[:, tile(n)], acc_up[:, tile(n)] = terms(grp, tile(n))
+
+    @pl.loop(0, hid_width // hid_tile)
+    def _(n):
+        for j in (1, 2):
+            take_tile(x_gg, gg_s, gg_r, n, j)
+            hand_on_tile(x_gg, gg_s, gg_r, n, j).start()
+            take_tile(x_gu, gu_s, gu_r, n, j)
+            hand_on_tile(x_gu, gu_s, gu_r, n, j).start()
+        for j in (1, 2):
+            gate, up = terms(paired(grp, j, groups), tile(n))
+            acc_gate[:, tile(n)] += gate
+            acc_up[:, tile(n)] += up
+
+    def combine(n):
+        for k in range(1, owners):
+            take_back(n, k)
+        gtok_ref[:, wide(n)] = dot_tn(
+            pick[...], back_recv[:, :, wide(n)].reshape(slots, wide_tile)
+        ).astype(BF16)
+
+    def finish(n):
+        for j in (1, 2):
+            take_on_tile(x_gg, gg_s, gg_r, n, j)
+            take_on_tile(x_gu, gu_s, gu_r, n, j)
+        gate, up = terms(paired(grp, 3, groups), tile(n))
+        gwg_ref[:, tile(n)] = (acc_gate[:, tile(n)] + gate).astype(BF16)
+        gwu_ref[:, tile(n)] = (acc_up[:, tile(n)] + up).astype(BF16)
+
+    pl.loop(0, width // wide_tile - 1)(combine)
+    pl.loop(0, hid_width // hid_tile - 1)(finish)
+    combine(width // wide_tile - 1)
 
     for k in range(1, owners):
-        take_block(back_send, back_recv, back_s, back_r, k)
         take_block(score_send, score_recv, sc_s, sc_r, k)
-
-    @pl.loop(0, width // wide_tile)
-    def _(n):
-        cols = pl.ds(pl.multiple_of(n * wide_tile, wide_tile), wide_tile)
-        gtok_ref[:, cols] = dot_tn(
-            pick[...], back_recv[:, :, cols].reshape(slots, wide_tile)
-        ).astype(BF16)
-
     first_sum = jnp.zeros((1, tok_count), F32)
     second_sum = jnp.zeros((1, tok_count), F32)
     for e in range(owners):
@@ -324,22 +363,29 @@
         )
         first_sum = first_sum + jnp.where(ids_ref[0:1, :] == e, by_token, 0.0)
         second_sum = second_sum + jnp.where(ids_ref[1:2, :] == e, by_token, 0.0)
-    ggate_ref[0:1, :] = first_sum / gates_ref[0:1, :]
-    ggate_ref[1:2, :] = second_sum / gates_ref[1:2, :]
-
-    for j in (1, 2):
-        take_on(x_gg, gg_s, gg_r, j)
-        take_on(x_gu, gu_s, gu_r, j)
-    add_group(paired(grp, 3, groups), False, True)
+    weights = gates_ref[...].astype(F32)
+    ggate_ref[...] = (jnp.concatenate([first_sum, second_sum], axis=0) / weights).astype(BF16)
+
+    finish(hid_width // hid_tile - 1)
 
     for k in range(1, owners):
         send_block(send_cot, scaled, cot_s, cot_r, k).wait_send()
-        send_block(back_send, back_recv, back_s, back_r, k).wait_send()
         send_block(score_send, score_recv, sc_s, sc_r, k).wait_send()
+    @pl.loop(0, width // wide_tile)
+    def _(n):
+        for k in range(1, owners):
+            send_back(n, k).wait_send()
+
+    @pl.loop(0, hid_width // hid_tile)
+    def _(n):
+        for j in (1, 2):
+            for held, send, recv in ((x_gg, gg_s, gg_r), (x_gu, gu_s, gu_r)):
+                spread_tile(held, send, recv, n, j).wait_send()
+                hand_on_tile(held, send, recv, n, j).wait_send()
+
     for j in (1, 2):
-        for held, send, recv in ((x_hid, h_s, h_r), (x_gg, gg_s, gg_r), (x_gu, gu_s, gu_r)):
-            spread(held, send, recv, j).wait_send()
-            hand_on(held, send, recv, j).wait_send()
+        spread(x_hid, h_s, h_r, j).wait_send()
+        hand_on(x_hid, h_s, h_r, j).wait_send()
     for j in range(1, groups):
         for k in range(owners):
             share(rows, x_rows, fr_s, fr_r, k, j).wait_send()
@@ -366,12 +412,14 @@
     parts = pltpu.VMEM((groups, owners, capacity, part), BF16)
     hids = pltpu.VMEM((groups, slots, hid_width), BF16)
     lines = pltpu.VMEM((owners, 8, 128), F32)
+    per_back = dma((width // tile_of(width, 512), owners))
+    per_tile = dma((hid_width // tile_of(hid_width, 256), groups))
     per_owner, per_group, per_share = dma((owners,)), dma((groups,)), dma((owners, groups))
     grad_tokens, grad_gates, grad_gate, grad_up, grad_down = pl.pallas_call(
         functools.partial(layer_kernel, owners, groups, capacity),
         out_shape=(
             jax.ShapeDtypeStruct((tok_rows, width), BF16),
-            jax.ShapeDtypeStruct((2, tok_rows), F32),
+            jax.ShapeDtypeStruct((2, tok_rows), BF16),
             jax.ShapeDtypeStruct((part, hid_width), BF16),
             jax.ShapeDtypeStruct((part, hid_width), BF16),
             jax.ShapeDtypeStruct((hid_width, part), BF16),
@@ -395,7 +443,8 @@
             pltpu.VMEM((part, hid_width), F32),
             pltpu.VMEM((part, hid_width), F32),
         ]
-        + [per_owner] * 8 + [per_share] * 4 + [per_group] * 6,
+        + [per_owner] * 4 + [per_back] * 2 + [per_owner] * 2 + [per_share] * 4
+        + [per_group] * 2 + [per_tile] * 4,
         compiler_params=pltpu.CompilerParams(
             collective_id=0, has_side_effects=True, vmem_limit_bytes=56 * 1024 * 1024
         ),
@@ -406,17 +455,17 @@
         ),
         name="expert_layer",
     )(
-        expert_ids.T, gates.astype(F32).T, tokens, cotangent, w_gate, w_up, w_down
-    )
-    held = (grad_tokens, grad_gate[None], grad_up[None], grad_down[None])
+        expert_ids.T, gates.T, tokens, cotangent, w_gate, w_up, w_down
+    )
+    held = (grad_tokens, grad_gates, grad_gate[None], grad_up[None], grad_down[None])
     quarters = [
-        pl.BlockSpec(
+        pl.BlockSpec(x.shape, lambda n: (0, 0)) if x.shape[0] == 2 else pl.BlockSpec(
             x.shape[:-2] + (x.shape[-2] // 4, x.shape[-1]),
             (lambda n: (n, 0)) if x.ndim == 2 else (lambda n: (0, n, 0)),
         )
         for x in held
     ]
-    grad_tokens, grad_gate, grad_up, grad_down = pl.pallas_call(
+    grad_tokens, grad_gates, grad_gate, grad_up, grad_down = pl.pallas_call(
         hand_over,
         grid=(4,),
         out_shape=tuple(jax.ShapeDtypeStruct(x.shape, x.dtype) for x in held),
@@ -424,7 +473,7 @@
         out_specs=tuple(quarters),
         name="hand_over",
     )(*held)
-    return (grad_tokens, grad_gates.T.astype(BF16), grad_gate, grad_up, grad_down)
+    return (grad_tokens, grad_gates.T, grad_gate, grad_up, grad_down)
 
 
 def contract_rows(left, right):

time: 137 us -> 134 us (0.978)
  other arithmetic: 2.39 us -> 0 us
where the time goes in v4:
time: 134 us
  Pallas kernels  133 us (99%)
    pallas_call x1, Pallas kernels, kernel_body(): pl.pallas_call(functools.partial(layer_kernel, owners, groups, capacity),...  129 us
    pallas_call x1, Pallas kernels, kernel_body(): pl.pallas_call(hand_over, grid=(4,), out_shape=tuple((jax.ShapeDtypeStruc...  4.14 us

profile of v4, /device:TPU:0, one launch (start us, length us, event | category | flops | bytes accessed | tf_op | source)
XLA Modules:
  0.0 133.8 jit_solution(14038776823509748374)
XLA Ops:
  0.6 129.0 %expert_layer.1 = (bf16[128,2048]{1,0:T(8,128)(2,1)}, bf16[2,128]{1,0:T(2,128)(2,1)}, bf16[512,768]{1,0:T(8,128)(2,1)}, bf16[512,768]{1,0:T(8,128)(2,1)}, bf16[768,512]{1,0:T(8,128)(2,1)}) custom-call(s32[2,128]{1,0:T(2,128)} %bitcast.9, bf16[2,128]{1,0:T(2,128)(2,1)} %bitcast.10, bf16[128,2048]{1,0:T(8,128)(2,1)} %tok_ref.1, bf16[128,2048]{1,0:T(8,128)(2,1)} %cot_ref.1, ...), custom_call_target="tpu_custom_call" | custom-call | flops 9663676416 | bytes 18874368 | tf_op jit(solution)/shard_map/expert_layer/pallas_call | solution.py:418
  129.6 4.1 %hand_over.1 = (bf16[128,2048]{1,0:T(8,128)(2,1)}, bf16[2,128]{1,0:T(2,128)(2,1)}, bf16[1,512,768]{2,1,0:T(8,128)(2,1)}, bf16[1,512,768]{2,1,0:T(8,128)(2,1)}, bf16[1,768,512]{2,1,0:T(8,128)(2,1)}) custom-call(bf16[128,2048]{1,0:T(8,128)(2,1)} %get-tuple-element.15.refs_0_, bf16[2,128]{1,0:T(2,128)(2,1)} %get-tuple-element.16.refs_1_, ...), custom_call_target="tpu_custom_call" | custom-call | tf_op jit(solution)/shard_map/hand_over/pallas_call | solution.py:468

commit v5 on v4

--- a/solution.py
+++ b/solution.py
@@ -195,6 +195,9 @@
         ).wait_recv()
 
     chip = lax.div(me, 2)
+    turn = lax.rem(me, 2)
+    near = (1 + turn, 2 - turn)
+    aside_order = near + (3,)
     inner = lax.rem(lax.div(chip + 1, 2), 2)
     out_order, in_order = [1], [1]
     for i in range(3):
@@ -213,13 +216,13 @@
 
     rows[me] = send_tok[me]
     scaled[me] = send_cot[me]
-    for j in range(1, groups):
+    for j in aside_order:
         share(rows, x_rows, fr_s, fr_r, 0, j).start()
     for out, k in zip(out_order, in_order):
         send_block(send_tok, rows, tok_s, tok_r, out).wait_send()
         send_block(send_cot, scaled, cot_s, cot_r, out).start()
         take_block(send_tok, rows, tok_s, tok_r, k)
-        for j in range(1, groups):
+        for j in aside_order:
             share(rows, x_rows, fr_s, fr_r, k, j).start()
 
     mine = pl.ds(pl.multiple_of(grp * part, part), part)
@@ -240,16 +243,16 @@
         gate_factor[:, cols] = up * sig * (1.0 + gate * (1.0 - sig))
         up_factor[:, cols] = active
 
-    for j in (1, 2):
+    for j in near:
         spread(x_hid, h_s, h_r, j).start()
-    for j in range(1, groups):
+    for j in aside_order:
         share(scaled, x_scaled, fc_s, fc_r, 0, j).start()
     for step, k in enumerate(in_order):
         take_block(send_cot, scaled, cot_s, cot_r, k)
-        for j in range(1, groups):
+        for j in aside_order:
             share(scaled, x_scaled, fc_s, fc_r, k, j).start()
         if step == owners // 2:
-            for j in (1, 2):
+            for j in near:
                 take_spread(x_hid, h_s, h_r, j)
                 hand_on(x_hid, h_s, h_r, j).start()
     own_scaled = pltpu.make_async_copy(scaled.at[:, :, mine], x_scaled.at[grp], own_sem.at[1])
@@ -263,7 +266,7 @@
         grad_hidden = dot_nt(scaled[...].reshape(slots, width), wd[cols, :])
         x_gg[grp, :, cols] = (grad_hidden * gate_factor[:, cols]).astype(BF16)
         x_gu[grp, :, cols] = (grad_hidden * up_factor[:, cols]).astype(BF16)
-        for j in (1, 2):
+        for j in near:
             spread_tile(x_gg, gg_s, gg_r, n, j).start()
             spread_tile(x_gu, gu_s, gu_r, n, j).start()
         score[...] += jnp.broadcast_to(
@@ -271,14 +274,24 @@
             (slots, 128),
         )
 
-    @pl.loop(0, width // wide_tile)
-    def _(n):
-        cols = pl.ds(pl.multiple_of(n * wide_tile, wide_tile), wide_tile)
+    def go_back(n):
+        cols = wide(n)
         grad = dot_nt(x_gg[grp], wg[cols, :]) + dot_nt(x_gu[grp], wu[cols, :])
         back_send[:, :, cols] = grad.astype(BF16).reshape(owners, capacity, wide_tile)
+        back_recv[me, :, cols] = back_send[me, :, cols]
+
+    def start_back(n):
         for k in out_order:
             send_back(n, k).start()
-        back_recv[me, :, cols] = back_send[me, :, cols]
+
+    wide_tiles, hid_tiles = width // wide_tile, hid_width // hid_tile
+
+    @pl.loop(0, wide_tiles // 2)
+    def _(n):
+        go_back(n)
+        start_back(n)
+
+    pl.loop(wide_tiles // 2, wide_tiles)(go_back)
 
     on_diagonal = lax.broadcasted_iota(jnp.int32, (capacity, 128), 0) == lax.broadcasted_iota(
         jnp.int32, (capacity, 128), 1
@@ -318,13 +331,20 @@
     def _(n):
         acc_gate[:, tile(n)], acc_up[:, tile(n)] = terms(grp, tile(n))
 
-    @pl.loop(0, hid_width // hid_tile)
-    def _(n):
-        for j in (1, 2):
+    @pl.loop(0, hid_tiles)
+    def _(n):
+        for j in near:
             take_tile(x_gg, gg_s, gg_r, n, j)
             hand_on_tile(x_gg, gg_s, gg_r, n, j).start()
             take_tile(x_gu, gu_s, gu_r, n, j)
             hand_on_tile(x_gu, gu_s, gu_r, n, j).start()
+        later = wide_tiles - wide_tiles // 2
+
+        @pl.loop(wide_tiles // 2 + (n * later + hid_tiles - 1) // hid_tiles,
+                 wide_tiles // 2 + ((n + 1) * later + hid_tiles - 1) // hid_tiles)
+        def _(m):
+            start_back(m)
+
         for j in (1, 2):
             gate, up = terms(paired(grp, j, groups), tile(n))
             acc_gate[:, tile(n)] += gate

time: 134 us -> 134 us (level)
  no operation moved by 1% of the time
where the time goes in v5:
time: 134 us
  Pallas kernels  133 us (99%)
    pallas_call x1, Pallas kernels, kernel_body(): pl.pallas_call(functools.partial(layer_kernel, owners, groups, capacity),...  129 us
    pallas_call x1, Pallas kernels, kernel_body(): pl.pallas_call(hand_over, grid=(4,), out_shape=tuple((jax.ShapeDtypeStruc...  4.14 us

profile of v5, /device:TPU:0, one launch (start us, length us, event | category | flops | bytes accessed | tf_op | source)
XLA Modules:
  0.0 133.8 jit_solution(9121569011794050247)
XLA Ops:
  0.6 129.0 %expert_layer.1 = (bf16[128,2048]{1,0:T(8,128)(2,1)}, bf16[2,128]{1,0:T(2,128)(2,1)}, bf16[512,768]{1,0:T(8,128)(2,1)}, bf16[512,768]{1,0:T(8,128)(2,1)}, bf16[768,512]{1,0:T(8,128)(2,1)}) custom-call(s32[2,128]{1,0:T(2,128)} %bitcast.9, bf16[2,128]{1,0:T(2,128)(2,1)} %bitcast.10, bf16[128,2048]{1,0:T(8,128)(2,1)} %tok_ref.1, bf16[128,2048]{1,0:T(8,128)(2,1)} %cot_ref.1, ...), custom_call_target="tpu_custom_call" | custom-call | flops 9663676416 | bytes 18874368 | tf_op jit(solution)/shard_map/expert_layer/pallas_call | solution.py:438
  129.6 4.1 %hand_over.1 = (bf16[128,2048]{1,0:T(8,128)(2,1)}, bf16[2,128]{1,0:T(2,128)(2,1)}, bf16[1,512,768]{2,1,0:T(8,128)(2,1)}, bf16[1,512,768]{2,1,0:T(8,128)(2,1)}, bf16[1,768,512]{2,1,0:T(8,128)(2,1)}) custom-call(bf16[128,2048]{1,0:T(8,128)(2,1)} %get-tuple-element.15.refs_0_, bf16[2,128]{1,0:T(2,128)(2,1)} %get-tuple-element.16.refs_1_, ...), custom_call_target="tpu_custom_call" | custom-call | tf_op jit(solution)/shard_map/hand_over/pallas_call | solution.py:488
